TPU v7x, 512 devices: a whole 4x4x16 slice. The times are simulated.
512 devices in a mesh: exp: 64 (over x, z), ctx: 8 (over y, core).
Axes of the slice: x: 4, y: 4, z: 16, core: 2. Of those that a mesh axis runs over, the one named last changes fastest.
Arguments:
- y_first: bfloat16 [8192, 1024], P('exp', 'ctx'), may hold values from -6 to 6
- y_second: bfloat16 [8192, 1024], P('exp', 'ctx'), may hold values from -6 to 6
- grad_first: bfloat16 [8192, 1024], P('exp', 'ctx'), may hold values from -6 to 6
- grad_second: bfloat16 [8192, 1024], P('exp', 'ctx'), may hold values from -6 to 6
- expert_ids: int32 [8192, 6], P('exp'), may hold values from 0 to 63, all different within a row; in each aligned block of 128 rows (0 to 127, 128 to 255, ...) at most 16 rows name the same one
- gate_fixed: int32 [8192, 6], P('exp'), may hold values from 4096 to 65535
- gain_attn: float32 [1024], replicated, may hold values from 0.5 to 1.5
- gain_latent: float32 [512], replicated, may hold values from 0.5 to 1.5
- gain_moe: float32 [1024], replicated, may hold values from 0.5 to 1.5
- w_query: bfloat16 [1024, 1024], P(None, 'ctx'), may hold values from -0.1875 to 0.1875
- w_latent: bfloat16 [1024, 512], P(None, 'ctx'), may hold values from -0.1875 to 0.1875
- w_key_up: bfloat16 [512, 1024], P(None, 'ctx'), may hold values from -0.25 to 0.25
- w_value_up: bfloat16 [512, 1024], P(None, 'ctx'), may hold values from -0.25 to 0.25
- w_out: bfloat16 [1024, 1024], P('ctx'), may hold values from -0.1875 to 0.1875
- w_gate: bfloat16 [64, 1024, 1408], P('exp', None, 'ctx'), may hold values from -0.1875 to 0.1875
- w_up: bfloat16 [64, 1024, 1408], P('exp', None, 'ctx'), may hold values from -0.1875 to 0.1875
- w_down: bfloat16 [64, 1408, 1024], P('exp', 'ctx'), may hold values from -0.15625 to 0.15625
Outputs:
- first_out: bfloat16 [8192, 1024], P('exp', 'ctx')
- second_out: bfloat16 [8192, 1024], P('exp', 'ctx')
- grad_first_out: bfloat16 [8192, 1024], P('exp', 'ctx')
- grad_second_out: bfloat16 [8192, 1024], P('exp', 'ctx')
Inputs may be any that keep to these rules, and one draw needn't show every extreme that they name: `expert_ids`: each row names 6 different experts. In each aligned block of 128 rows (one window, the rows of one index of exp) no expert is named by more than 16 rows, a bound that some expert reaches in every block.
All inputs are finite; a program needn't handle non-finite values.
Results may differ from a plain program's by a relative error of at most 0.025.
Values may be sent and summed in bfloat16 or wider, within the bound.
A program may use at most 64 MiB of HBM per device.

v0:
```python
import math
import jax
import jax.numpy as jnp
from jax import lax
from jax.sharding import PartitionSpec as P

HEAD_DIM = 128
TOP = 6
epsilon = 1e-06
soft_limit = 5.0


def rms_scale(row_data):
    return lax.rsqrt(jnp.mean(row_data * row_data, axis=-1, keepdims=True) + epsilon)


def rms_back(row_data, gain_vec, grad_in):
    factor = rms_scale(row_data)
    weighted = gain_vec * grad_in
    inner_mean = jnp.mean(weighted * row_data, axis=-1, keepdims=True)
    return factor * weighted - row_data * (factor * factor * factor) * inner_mean


def route_slots(expert_rows, expert_count):
    flat_ids = expert_rows.reshape(-1)
    labels = jnp.arange(expert_count)
    onehot = (flat_ids[:, None] == labels[None, :]).astype(jnp.int32)
    before = jnp.cumsum(onehot, axis=0) - onehot
    return jnp.sum(before * onehot, axis=1).reshape(expert_rows.shape)


def local(
    y_first,
    y_second,
    grad_first,
    grad_second,
    expert_ids,
    gate_fixed,
    gain_attn,
    gain_latent,
    gain_moe,
    w_query,
    w_latent,
    w_key_up,
    w_value_up,
    w_out,
    w_gate,
    w_up,
    w_down,
):
    ctx_count = lax.axis_size("ctx")
    exp_count = lax.axis_size("exp")
    ctx_index = lax.axis_index("ctx")
    local_experts = w_gate.shape[0]
    expert_count = exp_count * local_experts
    window_len = y_first.shape[0]
    own_cols = y_first.shape[1]
    model_width = own_cols * ctx_count
    capacity = ctx_count * (
        (window_len * TOP * 4 + 3 * expert_count * ctx_count - 1) // (3 * expert_count * ctx_count)
    )
    full_first, full_second, full_gfirst, full_gsecond = (
        lax.all_gather(y_first, "ctx", axis=1, tiled=True),
        lax.all_gather(y_second, "ctx", axis=1, tiled=True),
        lax.all_gather(grad_first, "ctx", axis=1, tiled=True),
        lax.all_gather(grad_second, "ctx", axis=1, tiled=True),
    )
    first_in = full_first.astype(jnp.float32)
    normed = (first_in * rms_scale(first_in) * gain_moe).astype(jnp.bfloat16)
    slot_ids = route_slots(expert_ids, expert_count)
    flat_slots = (expert_ids * capacity + slot_ids).reshape(-1)
    targets = jnp.arange(expert_count * capacity)
    hits = (targets[:, None] == flat_slots[None, :]).astype(jnp.bfloat16)
    chooser = jnp.max(hits.reshape(expert_count * capacity, window_len, TOP), axis=2)
    send_rows = jnp.dot(chooser, normed, preferred_element_type=jnp.float32).astype(jnp.bfloat16)
    send_rows = send_rows.reshape(expert_count, capacity, model_width)
    send_grads = jnp.dot(chooser, full_gsecond, preferred_element_type=jnp.float32).astype(
        jnp.bfloat16
    )
    send_grads = send_grads.reshape(expert_count, capacity, model_width)
    recv_rows, recv_grads = (
        lax.all_to_all(send_rows, "exp", split_axis=0, concat_axis=0, tiled=True),
        lax.all_to_all(send_grads, "exp", split_axis=0, concat_axis=0, tiled=True),
    )
    grouped_rows = recv_rows.reshape(exp_count, local_experts, capacity, model_width)
    grouped_grads = recv_grads.reshape(exp_count, local_experts, capacity, model_width)
    gate_proj = jnp.einsum(
        "secd,edf->secf", grouped_rows, w_gate, preferred_element_type=jnp.float32
    )
    up_proj = jnp.einsum("secd,edf->secf", grouped_rows, w_up, preferred_element_type=jnp.float32)
    sigmoid_gate = jax.nn.sigmoid(gate_proj)
    hidden = (gate_proj * sigmoid_gate * up_proj).astype(jnp.bfloat16)
    part_out = jnp.einsum(
        "secf,efd->secd", hidden, w_down, preferred_element_type=jnp.float32
    ).astype(jnp.bfloat16)
    grad_hidden = jnp.einsum(
        "secd,efd->secf", grouped_grads, w_down, preferred_element_type=jnp.float32
    )
    grad_gate = (
        grad_hidden * up_proj * sigmoid_gate * (1.0 + gate_proj * (1.0 - sigmoid_gate))
    ).astype(jnp.bfloat16)
    grad_up = (grad_hidden * gate_proj * sigmoid_gate).astype(jnp.bfloat16)
    part_back = jnp.einsum("secf,edf->secd", grad_gate, w_gate, preferred_element_type=jnp.float32)
    part_back = part_back + jnp.einsum(
        "secf,edf->secd", grad_up, w_up, preferred_element_type=jnp.float32
    )
    part_back = part_back.astype(jnp.bfloat16)
    weights = gate_fixed.astype(jnp.float32) / 65536.0
    back_out, back_grads = (
        lax.all_to_all(
            part_out.reshape(expert_count, capacity, model_width),
            "exp",
            split_axis=0,
            concat_axis=0,
            tiled=True,
        ),
        lax.all_to_all(
            part_back.reshape(expert_count, capacity, model_width),
            "exp",
            split_axis=0,
            concat_axis=0,
            tiled=True,
        ),
    )
    picked_out = jnp.take(
        back_out.reshape(expert_count * capacity, model_width), flat_slots, axis=0
    )
    picked_out = picked_out.reshape(window_len, TOP, model_width).astype(jnp.float32)
    picked_grads = jnp.take(
        back_grads.reshape(expert_count * capacity, model_width), flat_slots, axis=0
    )
    picked_grads = picked_grads.reshape(window_len, TOP, model_width).astype(jnp.float32)
    moe_part = jnp.sum(weights[:, :, None] * picked_out, axis=1)
    grad_part = jnp.sum(weights[:, :, None] * picked_grads, axis=1)
    moe_out, grad_moe = (
        lax.psum(moe_part.astype(jnp.bfloat16), "ctx").astype(jnp.float32),
        lax.psum(grad_part.astype(jnp.bfloat16), "ctx").astype(jnp.float32),
    )
    second_full = (full_second.astype(jnp.float32) - moe_out).astype(jnp.bfloat16)
    total_grad = full_gfirst.astype(jnp.float32) + rms_back(first_in, gain_moe, grad_moe)
    grad_first_full = total_grad.astype(jnp.bfloat16)
    second = second_full.astype(jnp.float32)
    attn_in = (second * rms_scale(second) * gain_attn).astype(jnp.bfloat16)
    queries = jnp.dot(attn_in, w_query, preferred_element_type=jnp.float32).astype(jnp.bfloat16)
    latent_part = jnp.dot(attn_in, w_latent, preferred_element_type=jnp.float32).astype(
        jnp.bfloat16
    )
    latent = lax.all_gather(latent_part, "ctx", axis=1, tiled=True)
    latent_f = latent.astype(jnp.float32)
    latent_norm = (latent_f * rms_scale(latent_f) * gain_latent).astype(jnp.bfloat16)
    key_rows = jnp.dot(latent_norm, w_key_up, preferred_element_type=jnp.float32).astype(
        jnp.bfloat16
    )
    value_rows = jnp.dot(latent_norm, w_value_up, preferred_element_type=jnp.float32).astype(
        jnp.bfloat16
    )
    local_heads = w_query.shape[1] // HEAD_DIM
    head_shape = (window_len, local_heads, HEAD_DIM)
    query_heads = queries.reshape(head_shape)
    key_heads = key_rows.reshape(head_shape)
    value_heads = value_rows.reshape(head_shape)
    scale_factor = 1.0 / math.sqrt(HEAD_DIM)
    raw_scores = (
        jnp.einsum("qhk,shk->hqs", query_heads, key_heads, preferred_element_type=jnp.float32)
        * scale_factor
    )
    bounded = jnp.tanh(raw_scores / soft_limit)
    positions = jnp.arange(window_len)
    allowed = positions[None, :] <= positions[:, None]
    exp_scores = jnp.where(allowed[None], jnp.exp(soft_limit * bounded), 0.0)
    probs_full = exp_scores / jnp.sum(exp_scores, axis=-1, keepdims=True)
    probs_low = probs_full.astype(jnp.bfloat16)
    mixed_heads = jnp.einsum(
        "hqs,shk->qhk", probs_low, value_heads, preferred_element_type=jnp.float32
    )
    mixed_heads = mixed_heads.astype(jnp.bfloat16).reshape(window_len, local_heads * HEAD_DIM)
    attn_part = jnp.dot(mixed_heads, w_out, preferred_element_type=jnp.float32)
    attn_out = lax.psum_scatter(
        attn_part.astype(jnp.bfloat16), "ctx", scatter_dimension=1, tiled=True
    ).astype(jnp.float32)
    first_out = (y_first.astype(jnp.float32) - attn_out).astype(jnp.bfloat16)
    grad_mixed = jnp.einsum(
        "td,hd->th", grad_first_full, w_out, preferred_element_type=jnp.float32
    ).astype(jnp.bfloat16)
    grad_heads = grad_mixed.reshape(head_shape)
    grad_probs = jnp.einsum(
        "qhk,shk->hqs", grad_heads, value_heads, preferred_element_type=jnp.float32
    )
    row_delta = jnp.sum(probs_full * grad_probs, axis=-1, keepdims=True)
    grad_scores = (
        probs_full * (grad_probs - row_delta) * (1.0 - bounded * bounded) * scale_factor
    ).astype(jnp.bfloat16)
    flat_width = local_heads * HEAD_DIM
    grad_queries = jnp.einsum(
        "hqs,shk->qhk", grad_scores, key_heads, preferred_element_type=jnp.float32
    )
    grad_queries = grad_queries.astype(jnp.bfloat16).reshape(window_len, flat_width)
    grad_keys = jnp.einsum(
        "hqs,qhk->shk", grad_scores, query_heads, preferred_element_type=jnp.float32
    )
    grad_keys = grad_keys.astype(jnp.bfloat16).reshape(window_len, flat_width)
    grad_values = jnp.einsum(
        "hqs,qhk->shk", probs_low, grad_heads, preferred_element_type=jnp.float32
    )
    grad_values = grad_values.astype(jnp.bfloat16).reshape(window_len, flat_width)
    latent_grad_part = jnp.einsum(
        "th,lh->tl", grad_keys, w_key_up, preferred_element_type=jnp.float32
    )
    latent_grad_part = latent_grad_part + jnp.einsum(
        "th,lh->tl", grad_values, w_value_up, preferred_element_type=jnp.float32
    )
    grad_latent_norm = lax.psum(latent_grad_part.astype(jnp.bfloat16), "ctx").astype(jnp.float32)
    grad_latent = rms_back(latent_f, gain_latent, grad_latent_norm).astype(jnp.bfloat16)
    latent_cols = w_latent.shape[1]
    own_latent = lax.dynamic_slice_in_dim(grad_latent, ctx_index * latent_cols, latent_cols, 1)
    input_part = jnp.einsum("th,dh->td", grad_queries, w_query, preferred_element_type=jnp.float32)
    input_part = input_part + jnp.einsum(
        "tl,dl->td", own_latent, w_latent, preferred_element_type=jnp.float32
    )
    grad_attn_in = lax.psum(input_part.astype(jnp.bfloat16), "ctx").astype(jnp.float32)
    full_back = rms_back(second, gain_attn, grad_attn_in)
    own_back = lax.dynamic_slice_in_dim(full_back, ctx_index * own_cols, own_cols, 1)
    grad_second_out = (grad_second.astype(jnp.float32) + own_back).astype(jnp.bfloat16)
    second_out = lax.dynamic_slice_in_dim(second_full, ctx_index * own_cols, own_cols, 1)
    grad_first_out = lax.dynamic_slice_in_dim(grad_first_full, ctx_index * own_cols, own_cols, 1)
    return (first_out, second_out, grad_first_out, grad_second_out)


def solution(mesh):
    placed = (
        P("exp", "ctx"),
        P("exp", "ctx"),
        P("exp", "ctx"),
        P("exp", "ctx"),
        P("exp", None),
        P("exp", None),
        P(),
        P(),
        P(),
        P(None, "ctx"),
        P(None, "ctx"),
        P(None, "ctx"),
        P(None, "ctx"),
        P("ctx", None),
        P("exp", None, "ctx"),
        P("exp", None, "ctx"),
        P("exp", "ctx", None),
    )
    return jax.shard_map(
        local,
        mesh=mesh,
        in_specs=placed,
        out_specs=(P("exp", "ctx"), P("exp", "ctx"), P("exp", "ctx"), P("exp", "ctx")),
        check_vma=False,
    )
```

profile of v0, /device:TPU:2, one launch (start us, length us, event | category | flops | bytes accessed | tf_op | source)
XLA Modules:
  0.0 782.4 jit_solution(9239729217433142094)
XLA Ops:
  11.8 12.6 %all_gather.16 = bf16[128,1024]{1,0:T(8,128)(2,1)S(1)} all-gather(bf16[128,128]{1,0:T(8,128)(2,1)} %param.19), channel_id=1, replica_groups=mesh['exp'=64,'ctx'=8] {'ctx'}, dimensions={1}, use_global_device_ids=true | all-gather | bytes 294912 | tf_op jit(solution)/shard_map/all_gather | solution.py:63
  27.3 18.8 %all-to-all-start = ((bf16[64,16,1024]{2,1,0:T(8,128)(2,1)}), bf16[64,16,1024]{2,1,0:T(8,128)(2,1)S(1)}, u32[]{:S(2)}, u32[]{:S(2)}) async-start(bf16[64,16,1024]{2,1,0:T(8,128)(2,1)} %bitcast.132), calls=%async_computation | async-start | bytes 4194304 | tf_op jit(solution)/shard_map/all_to_all | solution.py:82
  46.1 11.5 %all_gather.19 = bf16[128,1024]{1,0:T(8,128)(2,1)S(1)} all-gather(bf16[128,128]{1,0:T(8,128)(2,1)S(1)} %copy-done.11), channel_id=1, replica_groups=mesh['exp'=64,'ctx'=8] {'ctx'}, dimensions={1}, use_global_device_ids=true | all-gather | bytes 294912 | tf_op jit(solution)/shard_map/all_gather | solution.py:66
  59.6 82.4 %all-to-all-done = bf16[64,16,1024]{2,1,0:T(8,128)(2,1)S(1)} async-done(((bf16[64,16,1024]{2,1,0:T(8,128)(2,1)}), bf16[64,16,1024]{2,1,0:T(8,128)(2,1)S(1)}, u32[]{:S(2)}, u32[]{:S(2)}) %all-to-all-start) | async-done | bytes 2097184 | tf_op jit(solution)/shard_map/all_to_all | solution.py:82
  142.0 10.3 %all-to-all-start.2 = ((bf16[64,16,1024]{2,1,0:T(8,128)(2,1)}), bf16[64,16,1024]{2,1,0:T(8,128)(2,1)}, u32[]{:S(2)}, u32[]{:S(2)}) async-start(bf16[64,16,1024]{2,1,0:T(8,128)(2,1)} %bitcast.131), calls=%async_computation.2 | async-start | bytes 4194304 | tf_op jit(solution)/shard_map/all_to_all | solution.py:83
  155.1 94.1 %all-to-all-done.2 = bf16[64,16,1024]{2,1,0:T(8,128)(2,1)} async-done(((bf16[64,16,1024]{2,1,0:T(8,128)(2,1)}), bf16[64,16,1024]{2,1,0:T(8,128)(2,1)}, u32[]{:S(2)}, u32[]{:S(2)}) %all-to-all-start.2) | async-done | bytes 2097184 | tf_op jit(solution)/shard_map/all_to_all | solution.py:83
  249.2 2.3 convolution_bitcast_fusion
  254.7 8.8 %all-to-all-start.3 = ((bf16[64,16,1024]{2,1,0:T(8,128)(2,1)}), bf16[64,16,1024]{2,1,0:T(8,128)(2,1)S(1)}, u32[]{:S(2)}, u32[]{:S(2)}) async-start(bf16[64,16,1024]{2,1,0:T(8,128)(2,1)} %add_convert_fusion), calls=%async_computation.3 | async-start | bytes 4194304 | tf_op jit(solution)/shard_map/all_to_all | solution.py:117
  263.5 3.4 convolution_convert_fusion
  266.9 93.6 %all-to-all-done.3 = bf16[64,16,1024]{2,1,0:T(8,128)(2,1)S(1)} async-done(((bf16[64,16,1024]{2,1,0:T(8,128)(2,1)}), bf16[64,16,1024]{2,1,0:T(8,128)(2,1)S(1)}, u32[]{:S(2)}, u32[]{:S(2)}) %all-to-all-start.3) | async-done | bytes 2097184 | tf_op jit(solution)/shard_map/all_to_all | solution.py:117
  360.5 8.9 %all-to-all-start.1 = ((bf16[64,16,1024]{2,1,0:T(8,128)(2,1)}), bf16[64,16,1024]{2,1,0:T(8,128)(2,1)}, u32[]{:S(2)}, u32[]{:S(2)}) async-start(bf16[64,16,1024]{2,1,0:T(8,128)(2,1)} %convolution_convert_fusion), calls=%async_computation.1 | async-start | bytes 4194304 | tf_op jit(solution)/shard_map/all_to_all | solution.py:110
  370.7 3.6 gather_fusion.1
  374.3 92.0 %all-to-all-done.1 = bf16[64,16,1024]{2,1,0:T(8,128)(2,1)} async-done(((bf16[64,16,1024]{2,1,0:T(8,128)(2,1)}), bf16[64,16,1024]{2,1,0:T(8,128)(2,1)}, u32[]{:S(2)}, u32[]{:S(2)}) %all-to-all-start.1) | async-done | bytes 2097184 | tf_op jit(solution)/shard_map/all_to_all | solution.py:110
  466.3 6.4 gather_fusion
  472.7 4.0 select_convert_fusion.1
  476.7 4.6 reshape.255
  483.5 7.5 multiply_reduce_fusion
  491.2 11.6 %all_gather.18 = bf16[128,1024]{1,0:T(8,128)(2,1)S(1)} all-gather(bf16[128,128]{1,0:T(8,128)(2,1)S(1)} %copy-done.15), channel_id=1, replica_groups=mesh['exp'=64,'ctx'=8] {'ctx'}, dimensions={1}, use_global_device_ids=true | all-gather | bytes 294912 | tf_op jit(solution)/shard_map/all_gather | solution.py:65
  502.8 12.2 %all_gather.15 = bf16[128,1024]{1,0:T(8,128)(2,1)S(1)} all-gather(bf16[128,128]{1,0:T(8,128)(2,1)S(1)} %copy-done.16), channel_id=1, replica_groups=mesh['exp'=64,'ctx'=8] {'ctx'}, dimensions={1}, use_global_device_ids=true | all-gather | bytes 294912 | tf_op jit(solution)/shard_map/all_gather | solution.py:64
  515.0 45.9 %all-reduce.9.cloned.1.call-done = (bf16[128,1024]{1,0:T(8,128)(2,1)}, bf16[128,1024]{1,0:T(8,128)(2,1)}) async-done(((bf16[128,1024]{1,0:T(8,128)(2,1)}, bf16[128,1024]{1,0:T(8,128)(2,1)}), (bf16[128,1024]{1,0:T(8,128)(2,1)}, bf16[128,1024]{1,0:T(8,128)(2,1)})) %all-reduce.9.cloned.1.call-update) | async-done | bytes 524304 | tf_op jit(solution)/shard_map/psum | solution.py:136
  564.1 12.8 %all_gather.17 = bf16[128,512]{0,1:T(8,128)(2,1)S(1)} all-gather(bf16[128,64]{0,1:T(8,128)(2,1)S(1)} %convolution_convert_fusion.12), channel_id=1, replica_groups=mesh['exp'=64,'ctx'=8] {'ctx'}, dimensions={1}, use_global_device_ids=true | all-gather | bytes 147456 | tf_op jit(solution)/shard_map/all_gather | solution.py:148
  582.6 74.2 %all-reduce.5.cloned.1.call-done = bf16[128,512]{0,1:T(8,128)(2,1)} async-done(((bf16[128,512]{0,1:T(8,128)(2,1)}), bf16[128,512]{0,1:T(8,128)(2,1)}) %all-reduce.5.cloned.1.call-update) | async-done | bytes 131088 | tf_op jit(solution)/shard_map/psum | solution.py:212
  661.6 72.4 %all-reduce.7.cloned.1.call-done = bf16[128,1024]{1,0:T(8,128)(2,1)} async-done(((bf16[128,1024]{1,0:T(8,128)(2,1)}), bf16[128,1024]{1,0:T(8,128)(2,1)}) %all-reduce.7.cloned.1.call-update) | async-done | bytes 262160 | tf_op jit(solution)/shard_map/psum | solution.py:220
  735.9 38.4 %reduce-scatter.4.cloned.1.call-done = bf16[128,128]{1,0:T(8,128)(2,1)} async-done(((bf16[1024,128]{1,0:T(8,128)(2,1)}), bf16[128,128]{1,0:T(8,128)(2,1)}) %reduce-scatter.4.cloned.1.call-update) | async-done | bytes 32784
  (122 shorter events, 35.7 us)
Async XLA Ops:
  7.2 145.2 %copy-start = (bf16[1,1024,176]{1,2,0:T(8,128)(2,1)S(1)}, bf16[1,1024,176]{1,2,0:T(8,128)(2,1)}, u32[]{:S(2)}) copy-start(bf16[1,1024,176]{1,2,0:T(8,128)(2,1)} %param.33) | copy-start | bytes 1081348
  27.3 18.8 %copy-start.11 = (bf16[128,128]{1,0:T(8,128)(2,1)S(1)}, bf16[128,128]{1,0:T(8,128)(2,1)}, u32[]{:S(2)}) copy-start(bf16[128,128]{1,0:T(8,128)(2,1)} %param.22) | copy-start | bytes 98308
  27.3 114.7 %all-to-all-start = ((bf16[64,16,1024]{2,1,0:T(8,128)(2,1)}), bf16[64,16,1024]{2,1,0:T(8,128)(2,1)S(1)}, u32[]{:S(2)}, u32[]{:S(2)}) async-start(bf16[64,16,1024]{2,1,0:T(8,128)(2,1)} %bitcast.132), calls=%async_computation | async-start | bytes 4194304 | tf_op jit(solution)/shard_map/all_to_all | solution.py:82
  142.0 107.1 %all-to-all-start.2 = ((bf16[64,16,1024]{2,1,0:T(8,128)(2,1)}), bf16[64,16,1024]{2,1,0:T(8,128)(2,1)}, u32[]{:S(2)}, u32[]{:S(2)}) async-start(bf16[64,16,1024]{2,1,0:T(8,128)(2,1)} %bitcast.131), calls=%async_computation.2 | async-start | bytes 4194304 | tf_op jit(solution)/shard_map/all_to_all | solution.py:83
  155.1 96.4 %copy-start.3 = (f32[64,1,16,176]{3,2,0,1:T(8,128)S(1)}, f32[64,1,16,176]{3,2,0,1:T(8,128)}, u32[]{:S(2)}) copy-start(f32[64,1,16,176]{3,2,0,1:T(8,128)} %convolution_bitcast_fusion.1) | copy-start | bytes 2162692
  254.7 105.8 %all-to-all-start.3 = ((bf16[64,16,1024]{2,1,0:T(8,128)(2,1)}), bf16[64,16,1024]{2,1,0:T(8,128)(2,1)S(1)}, u32[]{:S(2)}, u32[]{:S(2)}) async-start(bf16[64,16,1024]{2,1,0:T(8,128)(2,1)} %add_convert_fusion), calls=%async_computation.3 | async-start | bytes 4194304 | tf_op jit(solution)/shard_map/all_to_all | solution.py:117
  266.9 103.0 %copy-start.19 = (s32[128,6]{0,1:T(8,128)S(1)}, s32[128,6]{0,1:T(8,128)}, u32[]{:S(2)}) copy-start(s32[128,6]{0,1:T(8,128)} %param.24) | copy-start | bytes 9220
  360.5 105.8 %all-to-all-start.1 = ((bf16[64,16,1024]{2,1,0:T(8,128)(2,1)}), bf16[64,16,1024]{2,1,0:T(8,128)(2,1)}, u32[]{:S(2)}, u32[]{:S(2)}) async-start(bf16[64,16,1024]{2,1,0:T(8,128)(2,1)} %convolution_convert_fusion), calls=%async_computation.1 | async-start | bytes 4194304 | tf_op jit(solution)/shard_map/all_to_all | solution.py:110
  369.4 191.5 %all-reduce.9.cloned.1.call-start = ((), (), s32[]{:S(2)}) async-start(), calls=%async_computation.8 | async-start | bytes 1048576 | tf_op jit(solution)/shard_map/psum | solution.py:136
  483.5 19.3 %copy-start.16 = (bf16[128,128]{1,0:T(8,128)(2,1)S(1)}, bf16[128,128]{1,0:T(8,128)(2,1)}, u32[]{:S(2)}) copy-start(bf16[128,128]{1,0:T(8,128)(2,1)} %param.20) | copy-start | bytes 98308
  483.5 77.4 %copy-start.2 = (bf16[128,1024]{1,0:T(8,128)(2,1)S(1)}, bf16[128,1024]{1,0:T(8,128)(2,1)}, u32[]{:S(2)}) copy-start(bf16[128,1024]{1,0:T(8,128)(2,1)} %copy-done.1) | copy-start | bytes 786436
  491.0 72.7 %copy-start.10 = (bf16[1024,64]{0,1:T(8,128)(2,1)S(1)}, bf16[1024,64]{0,1:T(8,128)(2,1)}, u32[]{:S(2)}) copy-start(bf16[1024,64]{0,1:T(8,128)(2,1)} %param.29) | copy-start | bytes 393220
  491.0 72.7 %copy-start.18 = (f32[1024]{0:T(1024)S(1)}, f32[1024]{0:T(1024)}, u32[]{:S(2)}) copy-start(f32[1024]{0:T(1024)} %param.25) | copy-start | bytes 12292
  491.0 86.4 %copy-start.8 = (bf16[1024,128]{1,0:T(8,128)(2,1)S(1)}, bf16[1024,128]{1,0:T(8,128)(2,1)}, u32[]{:S(2)}) copy-start(bf16[1024,128]{1,0:T(8,128)(2,1)} %param.28) | copy-start | bytes 786436
  491.1 165.7 %all-reduce.5.cloned.1.call-start = ((), (), s32[]{:S(2)}) async-start(), calls=%async_computation.5 | async-start | bytes 262144 | tf_op jit(solution)/shard_map/psum | solution.py:212
  491.1 86.6 %copy-start.9 = (bf16[512,128]{1,0:T(8,128)(2,1)S(1)}, bf16[512,128]{1,0:T(8,128)(2,1)}, u32[]{:S(2)}) copy-start(bf16[512,128]{1,0:T(8,128)(2,1)} %param.30) | copy-start | bytes 393220
  491.1 86.6 %copy-start.20 = (f32[512]{0:T(512)S(1)}, f32[512]{0:T(512)}, u32[]{:S(2)}) copy-start(f32[512]{0:T(512)} %param.26) | copy-start | bytes 6148
  502.8 75.3 %copy-start.13 = (bf16[512,128]{1,0:T(8,128)(2,1)S(1)}, bf16[512,128]{1,0:T(8,128)(2,1)}, u32[]{:S(2)}) copy-start(bf16[512,128]{1,0:T(8,128)(2,1)} %param.31) | copy-start | bytes 393220
  579.2 78.6 %copy-start.25 = (f32[128]{0:T(128)S(1)}, f32[128]{0:T(128)}, u32[]{:S(2)}) copy-start(f32[128]{0:T(128)} %get-tuple-element.19) | copy-start | bytes 1540
  582.0 152.0 %all-reduce.7.cloned.1.call-start = ((), (), s32[]{:S(2)}) async-start(), calls=%async_computation.6 | async-start | bytes 524288 | tf_op jit(solution)/shard_map/psum | solution.py:220
  582.5 152.7 %copy-start.22 = (f32[128]{0:T(128)S(1)}, f32[128]{0:T(128)}, u32[]{:S(2)}) copy-start(f32[128]{0:T(128)} %get-tuple-element.17) | copy-start | bytes 1540
  582.5 152.7 %copy-start.24 = (f32[128]{0:T(128)S(1)}, f32[128]{0:T(128)}, u32[]{:S(2)}) copy-start(f32[128]{0:T(128)} %copy-done.23) | copy-start | bytes 1540
  582.6 192.6 %copy-start.12 = (bf16[128,128]{1,0:T(8,128)(2,1)S(1)}, bf16[128,128]{1,0:T(8,128)(2,1)}, u32[]{:S(2)}) copy-start(bf16[128,128]{1,0:T(8,128)(2,1)} %param.19) | copy-start | bytes 98308
  659.5 114.8 %reduce-scatter.4.cloned.1.call-start = ((), (), s32[]{:S(2)}) async-start(), calls=%async_computation.7 | async-start | bytes 294912
  (11 other events, 96.3 us)
Sparse Core Ops, SparseCore 0:
  491.2 69.6 all-reduce.8
  582.1 74.5 all-reduce.4
  659.6 74.4 all-reduce.6
  736.9 37.3 reduce-scatter.3
where the time goes:
time: 783 us; the launch traced here: 782 us
  waiting for transfers between devices  593 us (76%)
  blocking collectives  60.7 us (8%)
  starting transfers between devices  47.2 us (6%)
  local copies, waits for them, and re-layouts  22.7 us (3%)
  other arithmetic  22.6 us (3%)
  matrix products  21.9 us (3%)
  between operations  14.2 us (2%)
    all_to_all x1, waiting for transfers between devices, local(): lax.all_to_all(send_grads, 'exp', split_axis=0, concat_axis=0, tiled=True)  94.1 us
    all_to_all x1, waiting for transfers between devices, local(): lax.all_to_all(part_back.reshape(expert_count, capacity, model_width), 'e...  93.6 us
    all_to_all x1, waiting for transfers between devices, local(): lax.all_to_all(part_out.reshape(expert_count, capacity, model_width), 'ex...  92 us
    all_to_all x1, waiting for transfers between devices, local(): lax.all_to_all(send_rows, 'exp', split_axis=0, concat_axis=0, tiled=True)  82.4 us
    psum x1, waiting for transfers between devices, local(): lax.psum(latent_grad_part.astype(jnp.bfloat16), 'ctx').astype(jnp.float32)  74.2 us
    psum x1, waiting for transfers between devices, local(): lax.psum(input_part.astype(jnp.bfloat16), 'ctx').astype(jnp.float32)  72.4 us
    psum x1, waiting for transfers between devices, local(): lax.psum(moe_part.astype(jnp.bfloat16), 'ctx').astype(jnp.float32)  45.9 us
    unnamed x5, waiting for transfers between devices  38.4 us
  transfers between devices with their start and end apart: 8, of which 8 were waited for; matrix products, arithmetic and copies ran while one was open for 2% of the time, Pallas kernels for 0%

commit v1 on v0

--- a/solution.py
+++ b/solution.py
@@ -133,7 +133,7 @@
     moe_part = jnp.sum(weights[:, :, None] * picked_out, axis=1)
     grad_part = jnp.sum(weights[:, :, None] * picked_grads, axis=1)
     moe_out, grad_moe = (
-        lax.psum(moe_part.astype(jnp.bfloat16), "ctx").astype(jnp.float32),
+        jnp.sum(lax.all_gather(moe_part.astype(jnp.bfloat16), "ctx"), axis=0).astype(jnp.float32),
         lax.psum(grad_part.astype(jnp.bfloat16), "ctx").astype(jnp.float32),
     )
     second_full = (full_second.astype(jnp.float32) - moe_out).astype(jnp.bfloat16)

time: 783 us -> 814 us (1.040)
  waiting for transfers between devices: 593 us -> 624 us
    all_gather x0 -> x1, waiting for transfers between devices: none -> 31.2 us  [local(): lax.all_gather(moe_part.astype(jnp.bfloat16), 'ctx')]
    unnamed x5 -> x6, waiting for transfers between devices: 38.4 us -> 39.2 us
  transfers between devices with their start and end apart: 8 -> 9, of which waited for: 8 -> 9; matrix products, arithmetic and copies ran while one was open for 2% -> 2% of each run, Pallas kernels for 0% -> 0%
where the time goes in v1:
time: 814 us; the launch traced here: 813 us
  waiting for transfers between devices  624 us (77%)
  blocking collectives  60.1 us (7%)
  starting transfers between devices  47.2 us (6%)
  local copies, waits for them, and re-layouts  23.2 us (3%)
  other arithmetic  23 us (3%)
  matrix products  20.5 us (3%)
  between operations  14.2 us (2%)
    all_to_all x1, waiting for transfers between devices, local(): lax.all_to_all(send_grads, 'exp', split_axis=0, concat_axis=0, tiled=True)  94.1 us
    all_to_all x1, waiting for transfers between devices, local(): lax.all_to_all(part_back.reshape(expert_count, capacity, model_width), 'e...  93.6 us
    all_to_all x1, waiting for transfers between devices, local(): lax.all_to_all(part_out.reshape(expert_count, capacity, model_width), 'ex...  92 us
    all_to_all x1, waiting for transfers between devices, local(): lax.all_to_all(send_rows, 'exp', split_axis=0, concat_axis=0, tiled=True)  82.4 us
    psum x1, waiting for transfers between devices, local(): lax.psum(latent_grad_part.astype(jnp.bfloat16), 'ctx').astype(jnp.float32)  74.5 us
    psum x1, waiting for transfers between devices, local(): lax.psum(input_part.astype(jnp.bfloat16), 'ctx').astype(jnp.float32)  72.6 us
    psum x1, waiting for transfers between devices, local(): lax.psum(grad_part.astype(jnp.bfloat16), 'ctx').astype(jnp.float32)  44.9 us
    unnamed x6, waiting for transfers between devices  39.2 us
  transfers between devices with their start and end apart: 9, of which 9 were waited for; matrix products, arithmetic and copies ran while one was open for 2% of the time, Pallas kernels for 0%

profile of v1, /device:TPU:2, one launch (start us, length us, event | category | flops | bytes accessed | tf_op | source)
XLA Modules:
  0.0 812.5 jit_solution(13778810139765253252)
XLA Ops:
  11.8 12.6 %all_gather.20 = bf16[128,1024]{1,0:T(8,128)(2,1)S(1)} all-gather(bf16[128,128]{1,0:T(8,128)(2,1)} %param.19), channel_id=1, replica_groups=mesh['exp'=64,'ctx'=8] {'ctx'}, dimensions={1}, use_global_device_ids=true | all-gather | bytes 294912 | tf_op jit(solution)/shard_map/all_gather | solution.py:63
  27.3 18.8 %all-to-all-start = ((bf16[64,16,1024]{2,1,0:T(8,128)(2,1)}), bf16[64,16,1024]{2,1,0:T(8,128)(2,1)S(1)}, u32[]{:S(2)}, u32[]{:S(2)}) async-start(bf16[64,16,1024]{2,1,0:T(8,128)(2,1)} %bitcast.133), calls=%async_computation | async-start | bytes 4194304 | tf_op jit(solution)/shard_map/all_to_all | solution.py:82
  46.1 11.5 %all_gather.24 = bf16[128,1024]{1,0:T(8,128)(2,1)S(1)} all-gather(bf16[128,128]{1,0:T(8,128)(2,1)S(1)} %copy-done.10), channel_id=1, replica_groups=mesh['exp'=64,'ctx'=8] {'ctx'}, dimensions={1}, use_global_device_ids=true | all-gather | bytes 294912 | tf_op jit(solution)/shard_map/all_gather | solution.py:66
  59.6 82.4 %all-to-all-done = bf16[64,16,1024]{2,1,0:T(8,128)(2,1)S(1)} async-done(((bf16[64,16,1024]{2,1,0:T(8,128)(2,1)}), bf16[64,16,1024]{2,1,0:T(8,128)(2,1)S(1)}, u32[]{:S(2)}, u32[]{:S(2)}) %all-to-all-start) | async-done | bytes 2097184 | tf_op jit(solution)/shard_map/all_to_all | solution.py:82
  142.0 10.3 %all-to-all-start.2 = ((bf16[64,16,1024]{2,1,0:T(8,128)(2,1)}), bf16[64,16,1024]{2,1,0:T(8,128)(2,1)}, u32[]{:S(2)}, u32[]{:S(2)}) async-start(bf16[64,16,1024]{2,1,0:T(8,128)(2,1)} %bitcast.132), calls=%async_computation.2 | async-start | bytes 4194304 | tf_op jit(solution)/shard_map/all_to_all | solution.py:83
  155.1 94.1 %all-to-all-done.2 = bf16[64,16,1024]{2,1,0:T(8,128)(2,1)} async-done(((bf16[64,16,1024]{2,1,0:T(8,128)(2,1)}), bf16[64,16,1024]{2,1,0:T(8,128)(2,1)}, u32[]{:S(2)}, u32[]{:S(2)}) %all-to-all-start.2) | async-done | bytes 2097184 | tf_op jit(solution)/shard_map/all_to_all | solution.py:83
  254.7 8.8 %all-to-all-start.3 = ((bf16[64,16,1024]{2,1,0:T(8,128)(2,1)}), bf16[64,16,1024]{2,1,0:T(8,128)(2,1)S(1)}, u32[]{:S(2)}, u32[]{:S(2)}) async-start(bf16[64,16,1024]{2,1,0:T(8,128)(2,1)} %add_convert_fusion), calls=%async_computation.3 | async-start | bytes 4194304 | tf_op jit(solution)/shard_map/all_to_all | solution.py:117
  263.5 3.4 convolution_convert_fusion
  266.9 93.6 %all-to-all-done.3 = bf16[64,16,1024]{2,1,0:T(8,128)(2,1)S(1)} async-done(((bf16[64,16,1024]{2,1,0:T(8,128)(2,1)}), bf16[64,16,1024]{2,1,0:T(8,128)(2,1)S(1)}, u32[]{:S(2)}, u32[]{:S(2)}) %all-to-all-start.3) | async-done | bytes 2097184 | tf_op jit(solution)/shard_map/all_to_all | solution.py:117
  360.5 8.9 %all-to-all-start.1 = ((bf16[64,16,1024]{2,1,0:T(8,128)(2,1)}), bf16[64,16,1024]{2,1,0:T(8,128)(2,1)}, u32[]{:S(2)}, u32[]{:S(2)}) async-start(bf16[64,16,1024]{2,1,0:T(8,128)(2,1)} %convolution_convert_fusion), calls=%async_computation.1 | async-start | bytes 4194304 | tf_op jit(solution)/shard_map/all_to_all | solution.py:110
  370.6 3.6 gather_fusion.1
  374.2 92.0 %all-to-all-done.1 = bf16[64,16,1024]{2,1,0:T(8,128)(2,1)} async-done(((bf16[64,16,1024]{2,1,0:T(8,128)(2,1)}), bf16[64,16,1024]{2,1,0:T(8,128)(2,1)}, u32[]{:S(2)}, u32[]{:S(2)}) %all-to-all-start.1) | async-done | bytes 2097184 | tf_op jit(solution)/shard_map/all_to_all | solution.py:110
  466.3 6.4 gather_fusion
  472.7 4.0 select_convert_fusion.1
  476.7 4.6 reshape.263
  483.5 7.5 multiply_reduce_fusion
  491.8 11.5 %all_gather.23 = bf16[128,1024]{1,0:T(8,128)(2,1)S(1)} all-gather(bf16[128,128]{1,0:T(8,128)(2,1)S(1)} %copy-done.14), channel_id=1, replica_groups=mesh['exp'=64,'ctx'=8] {'ctx'}, dimensions={1}, use_global_device_ids=true | all-gather | bytes 294912 | tf_op jit(solution)/shard_map/all_gather | solution.py:65
  503.4 11.6 %all_gather.19 = bf16[128,1024]{1,0:T(8,128)(2,1)S(1)} all-gather(bf16[128,128]{1,0:T(8,128)(2,1)S(1)} %copy-done.15), channel_id=1, replica_groups=mesh['exp'=64,'ctx'=8] {'ctx'}, dimensions={1}, use_global_device_ids=true | all-gather | bytes 294912 | tf_op jit(solution)/shard_map/all_gather | solution.py:64
  515.0 44.9 %all-reduce.4.cloned.1.call-done = bf16[128,1024]{1,0:T(8,128)(2,1)} async-done(((bf16[128,1024]{1,0:T(8,128)(2,1)}), bf16[128,1024]{1,0:T(8,128)(2,1)}) %all-reduce.4.cloned.1.call-update) | async-done | bytes 262160 | tf_op jit(solution)/shard_map/psum | solution.py:137
  563.1 31.2 %all-gather.3.cloned.1.call-done = bf16[1024,1024]{1,0:T(8,128)(2,1)} async-done(((bf16[128,1024]{1,0:T(8,128)(2,1)}), bf16[1024,1024]{1,0:T(8,128)(2,1)}) %all-gather.3.cloned.1.call-update) | async-done | bytes 2097168 | tf_op jit(solution)/shard_map/all_gather | solution.py:136
  596.9 12.8 %all_gather.22 = bf16[128,512]{0,1:T(8,128)(2,1)S(1)} all-gather(bf16[128,64]{0,1:T(8,128)(2,1)S(1)} %convolution_convert_fusion.12), channel_id=1, replica_groups=mesh['exp'=64,'ctx'=8] {'ctx'}, dimensions={1}, use_global_device_ids=true | all-gather | bytes 147456 | tf_op jit(solution)/shard_map/all_gather | solution.py:148
  613.1 74.5 %all-reduce.6.cloned.1.call-done = bf16[128,512]{0,1:T(8,128)(2,1)} async-done(((bf16[128,512]{0,1:T(8,128)(2,1)}), bf16[128,512]{0,1:T(8,128)(2,1)}) %all-reduce.6.cloned.1.call-update) | async-done | bytes 131088 | tf_op jit(solution)/shard_map/psum | solution.py:212
  691.6 72.6 %all-reduce.8.cloned.1.call-done = bf16[128,1024]{1,0:T(8,128)(2,1)} async-done(((bf16[128,1024]{1,0:T(8,128)(2,1)}), bf16[128,1024]{1,0:T(8,128)(2,1)}) %all-reduce.8.cloned.1.call-update) | async-done | bytes 262160 | tf_op jit(solution)/shard_map/psum | solution.py:220
  766.1 38.4 %reduce-scatter.4.cloned.1.call-done = bf16[128,128]{1,0:T(8,128)(2,1)} async-done(((bf16[1024,128]{1,0:T(8,128)(2,1)}), bf16[128,128]{1,0:T(8,128)(2,1)}) %reduce-scatter.4.cloned.1.call-update) | async-done | bytes 32784
  (110 shorter events, 38.3 us)
Async XLA Ops:
  7.2 145.2 %copy-start = (bf16[1,1024,176]{1,2,0:T(8,128)(2,1)S(1)}, bf16[1,1024,176]{1,2,0:T(8,128)(2,1)}, u32[]{:S(2)}) copy-start(bf16[1,1024,176]{1,2,0:T(8,128)(2,1)} %param.33) | copy-start | bytes 1081348
  7.2 18.0 %copy-start.13 = (f32[1024]{0:T(1024)S(1)}, f32[1024]{0:T(1024)}, u32[]{:S(2)}) copy-start(f32[1024]{0:T(1024)} %param.27) | copy-start | bytes 12292
  27.3 18.8 %copy-start.10 = (bf16[128,128]{1,0:T(8,128)(2,1)S(1)}, bf16[128,128]{1,0:T(8,128)(2,1)}, u32[]{:S(2)}) copy-start(bf16[128,128]{1,0:T(8,128)(2,1)} %param.22) | copy-start | bytes 98308
  27.3 114.7 %all-to-all-start = ((bf16[64,16,1024]{2,1,0:T(8,128)(2,1)}), bf16[64,16,1024]{2,1,0:T(8,128)(2,1)S(1)}, u32[]{:S(2)}, u32[]{:S(2)}) async-start(bf16[64,16,1024]{2,1,0:T(8,128)(2,1)} %bitcast.133), calls=%async_computation | async-start | bytes 4194304 | tf_op jit(solution)/shard_map/all_to_all | solution.py:82
  142.0 107.1 %all-to-all-start.2 = ((bf16[64,16,1024]{2,1,0:T(8,128)(2,1)}), bf16[64,16,1024]{2,1,0:T(8,128)(2,1)}, u32[]{:S(2)}, u32[]{:S(2)}) async-start(bf16[64,16,1024]{2,1,0:T(8,128)(2,1)} %bitcast.132), calls=%async_computation.2 | async-start | bytes 4194304 | tf_op jit(solution)/shard_map/all_to_all | solution.py:83
  155.1 96.5 %copy-start.3 = (f32[64,1,16,176]{3,2,0,1:T(8,128)S(1)}, f32[64,1,16,176]{3,2,0,1:T(8,128)}, u32[]{:S(2)}) copy-start(f32[64,1,16,176]{3,2,0,1:T(8,128)} %convolution_bitcast_fusion.1) | copy-start | bytes 2162692
  254.7 105.8 %all-to-all-start.3 = ((bf16[64,16,1024]{2,1,0:T(8,128)(2,1)}), bf16[64,16,1024]{2,1,0:T(8,128)(2,1)S(1)}, u32[]{:S(2)}, u32[]{:S(2)}) async-start(bf16[64,16,1024]{2,1,0:T(8,128)(2,1)} %add_convert_fusion), calls=%async_computation.3 | async-start | bytes 4194304 | tf_op jit(solution)/shard_map/all_to_all | solution.py:117
  266.9 102.9 %copy-start.17 = (s32[128,6]{0,1:T(8,128)S(1)}, s32[128,6]{0,1:T(8,128)}, u32[]{:S(2)}) copy-start(s32[128,6]{0,1:T(8,128)} %param.24) | copy-start | bytes 9220
  360.5 105.8 %all-to-all-start.1 = ((bf16[64,16,1024]{2,1,0:T(8,128)(2,1)}), bf16[64,16,1024]{2,1,0:T(8,128)(2,1)}, u32[]{:S(2)}, u32[]{:S(2)}) async-start(bf16[64,16,1024]{2,1,0:T(8,128)(2,1)} %convolution_convert_fusion), calls=%async_computation.1 | async-start | bytes 4194304 | tf_op jit(solution)/shard_map/all_to_all | solution.py:110
  369.4 190.5 %all-reduce.4.cloned.1.call-start = ((), (), s32[]{:S(2)}) async-start(), calls=%async_computation.5 | async-start | bytes 524288 | tf_op jit(solution)/shard_map/psum | solution.py:137
  483.5 19.9 %copy-start.15 = (bf16[128,128]{1,0:T(8,128)(2,1)S(1)}, bf16[128,128]{1,0:T(8,128)(2,1)}, u32[]{:S(2)}) copy-start(bf16[128,128]{1,0:T(8,128)(2,1)} %param.20) | copy-start | bytes 98308
  483.5 76.4 %copy-start.2 = (bf16[128,1024]{1,0:T(8,128)(2,1)S(1)}, bf16[128,1024]{1,0:T(8,128)(2,1)}, u32[]{:S(2)}) copy-start(bf16[128,1024]{1,0:T(8,128)(2,1)} %copy-done.1) | copy-start | bytes 786436
  491.0 71.8 %copy-start.6 = (bf16[128,1024]{1,0:T(8,128)(2,1)S(1)}, bf16[128,1024]{1,0:T(8,128)(2,1)}, u32[]{:S(2)}) copy-start(bf16[128,1024]{1,0:T(8,128)(2,1)} %param.32) | copy-start | bytes 786436
  491.0 103.3 %all-gather.3.cloned.1.call-start = ((), (), s32[]{:S(2)}) async-start(), calls=%async_computation.8 | async-start | bytes 2359296 | tf_op jit(solution)/shard_map/all_gather | solution.py:136
  491.8 195.8 %all-reduce.6.cloned.1.call-start = ((), (), s32[]{:S(2)}) async-start(), calls=%async_computation.6 | async-start | bytes 262144 | tf_op jit(solution)/shard_map/psum | solution.py:212
  563.0 33.5 %copy-start.9 = (bf16[1024,64]{0,1:T(8,128)(2,1)S(1)}, bf16[1024,64]{0,1:T(8,128)(2,1)}, u32[]{:S(2)}) copy-start(bf16[1024,64]{0,1:T(8,128)(2,1)} %param.29) | copy-start | bytes 393220
  563.1 33.5 %copy-start.16 = (f32[1024]{0:T(1024)S(1)}, f32[1024]{0:T(1024)}, u32[]{:S(2)}) copy-start(f32[1024]{0:T(1024)} %param.25) | copy-start | bytes 12292
  594.3 15.4 %copy-start.7 = (bf16[1024,128]{1,0:T(8,128)(2,1)S(1)}, bf16[1024,128]{1,0:T(8,128)(2,1)}, u32[]{:S(2)}) copy-start(bf16[1024,128]{1,0:T(8,128)(2,1)} %param.28) | copy-start | bytes 786436
  596.3 13.7 %copy-start.8 = (bf16[512,128]{1,0:T(8,128)(2,1)S(1)}, bf16[512,128]{1,0:T(8,128)(2,1)}, u32[]{:S(2)}) copy-start(bf16[512,128]{1,0:T(8,128)(2,1)} %param.30) | copy-start | bytes 393220
  596.3 13.7 %copy-start.18 = (f32[512]{0:T(512)S(1)}, f32[512]{0:T(512)}, u32[]{:S(2)}) copy-start(f32[512]{0:T(512)} %param.26) | copy-start | bytes 6148
  596.3 14.1 %copy-start.12 = (bf16[512,128]{1,0:T(8,128)(2,1)S(1)}, bf16[512,128]{1,0:T(8,128)(2,1)}, u32[]{:S(2)}) copy-start(bf16[512,128]{1,0:T(8,128)(2,1)} %param.31) | copy-start | bytes 393220
  612.6 151.6 %all-reduce.8.cloned.1.call-start = ((), (), s32[]{:S(2)}) async-start(), calls=%async_computation.7 | async-start | bytes 524288 | tf_op jit(solution)/shard_map/psum | solution.py:220
  688.7 116.7 %copy-start.11 = (bf16[128,128]{1,0:T(8,128)(2,1)S(1)}, bf16[128,128]{1,0:T(8,128)(2,1)}, u32[]{:S(2)}) copy-start(bf16[128,128]{1,0:T(8,128)(2,1)} %param.19) | copy-start | bytes 98308
  689.7 114.8 %reduce-scatter.4.cloned.1.call-start = ((), (), s32[]{:S(2)}) async-start(), calls=%async_computation.9 | async-start | bytes 294912
  (4 other events, 11.1 us)
Sparse Core Ops, SparseCore 0:
  491.2 68.6 all-reduce.3
  562.2 32.0 all-gather.2
  612.7 74.8 all-reduce.5
  689.8 74.4 all-reduce.7
  767.1 37.3 reduce-scatter.3
